TPU v7x, 512 devices: a whole 4x8x8 slice. The times are simulated.
512 devices in a mesh: replica: 64 (over y_hi, z, core), tp: 8 (over y_lo, x).
Axes of the slice: x: 4, y: 8 (y_hi: 4, y_lo: 2; y = y_hi * 2 + y_lo), z: 8, core: 2. Of those that a mesh axis runs over, the one named last changes fastest.
Arguments:
- queries: bfloat16 [256, 32, 128], P('replica', 'tp'), may hold values from -14 to 14
- key_new: bfloat16 [256, 8, 128], P('replica', 'tp'), may hold values from -7.2 to 7.2
- new_token_value: bfloat16 [256, 8, 128], P('replica', 'tp'), may hold values from -6 to 6
- key_pool: bfloat16 [512, 8, 128, 128], P('replica', 'tp'), may hold values from -4 to 4
- value_block_pool: bfloat16 [512, 8, 128, 128], P('replica', 'tp'), may hold values from -6 to 6
- block_table: int32 [256, 2], P('replica'), may hold values from 0 to 7, as said below
- cache_blocks: int32 [256], P('replica'), may hold values from 1 to 2, as said below
- mig_request: int32 [128], P('replica'), may hold values from 0 to 3, as said below
- mig_dest: int32 [128], P('replica'), may hold values from 0 to 63, as said below
- levels: bfloat16 [4096, 4096], P('tp'), may hold values from -127 to 127, as said below
- chan_scale: float32 [4096], P('tp'), may hold values from 0.001 to 0.01
- residual: bfloat16 [256, 4096], P('replica', 'tp'), may hold values from -24 to 24
- norm_gain: float32 [4096], P('tp'), may hold values from 0.5 to 1.5
Outputs:
- hidden: bfloat16 [256, 4096], P('replica', 'tp')
- normed: bfloat16 [256, 4096], P('replica', 'tp')
- recv_key: bfloat16 [128, 2, 8, 128, 128], P('replica', None, 'tp')
- recv_value: bfloat16 [128, 2, 8, 128, 128], P('replica', None, 'tp')
- recv_count: int32 [128], P('replica')
- recv_source: int32 [128], P('replica')
Inputs may be any that keep to these rules, and one draw needn't show every extreme that they name: `block_table`: the 4 x 2 entries of one replica name each of its 8 pool blocks once. `cache_blocks`: every replica has a request with 2 blocks. `mig_request`: the 2 entries of one replica name different requests; some replica lists a request with 2 blocks. `mig_dest`: for each j, entry j of the 64 replicas names every replica exactly once, and no replica names itself. `levels`: whole numbers.
All inputs are finite; a program needn't handle non-finite values.
Results may differ from a plain program's by a relative error of at most 0.024.
Values may be sent and summed in bfloat16 or wider, within the bound.
A program may use at most 128 MiB of HBM per device.

v0:
```python
import math

import jax
import jax.numpy as jnp
from jax import lax
from jax.sharding import PartitionSpec as P

DW = 4096
BLOCK_TOKENS = 128
MAX_BLOCK_COUNT = 2
MIGS = 2


def attend(queries, key_new, new_token_value, keys, values, cache_blocks):
    request_rows, kv_heads, span, width = keys.shape
    grouped_heads = queries.reshape(request_rows, kv_heads, -1, width)
    scale = 1.0 / math.sqrt(width)
    scores = (
        jnp.einsum("rkgd,rktd->rkgt", grouped_heads, keys, preferred_element_type=jnp.float32)
        * scale
    )
    own = (
        jnp.einsum("rkgd,rkd->rkg", grouped_heads, key_new, preferred_element_type=jnp.float32)
        * scale
    )
    live = jnp.arange(span, dtype=jnp.int32)[None, :] < (cache_blocks * BLOCK_TOKENS)[:, None]
    live = live[:, None, None, :]
    masked = jnp.where(live, scores, jnp.float32(-1e30))
    top = jnp.maximum(jnp.max(masked, axis=-1), own)
    expo = jnp.where(live, jnp.exp(masked - top[..., None]), jnp.float32(0.0))
    self_expo = jnp.exp(own - top)
    total = jnp.sum(expo, axis=-1) + self_expo
    weights = (expo / total[..., None]).astype(jnp.bfloat16)
    self_weight = (self_expo / total).astype(jnp.bfloat16)
    mixed = jnp.einsum("rkgt,rktd->rkgd", weights, values, preferred_element_type=jnp.float32)
    mixed = (
        mixed
        + self_weight.astype(jnp.float32)[..., None]
        * new_token_value.astype(jnp.float32)[:, :, None, :]
    )
    return mixed.reshape(request_rows, -1).astype(jnp.bfloat16)


def cached_blocks(block_pool, block_table):
    request_rows, depth = block_table.shape
    picked_blocks = jnp.take(block_pool, block_table.reshape(-1), axis=0)
    picked_blocks = picked_blocks.reshape((request_rows, depth) + block_pool.shape[1:])
    picked_blocks = jnp.transpose(picked_blocks, (0, 2, 1, 3, 4))
    return picked_blocks.reshape(
        request_rows, block_pool.shape[1], depth * block_pool.shape[2], block_pool.shape[3]
    )


def outgoing_blocks(block_pool, block_tables, live):
    picked_blocks = jnp.take(block_pool, block_tables.reshape(-1), axis=0)
    picked_blocks = picked_blocks.reshape(
        (block_tables.shape[0], block_tables.shape[1]) + block_pool.shape[1:]
    )
    picked_blocks = jnp.where(
        live[:, :, None, None, None], picked_blocks, jnp.zeros_like(picked_blocks)
    )
    return picked_blocks.reshape(block_tables.shape[0], -1)


def shards(
    queries,
    key_new,
    new_token_value,
    key_pool,
    value_block_pool,
    block_table,
    cache_blocks,
    mig_request,
    mig_dest,
    levels,
    chan_scale,
    residual,
    norm_gain,
):
    attn = attend(
        queries,
        key_new,
        new_token_value,
        cached_blocks(key_pool, block_table),
        cached_blocks(value_block_pool, block_table),
        cache_blocks,
    )
    partial_sums = jnp.dot(attn, levels, preferred_element_type=jnp.float32)
    summed = lax.psum_scatter(
        partial_sums.astype(jnp.bfloat16), "tp", scatter_dimension=1, tiled=True
    ).astype(jnp.float32)
    hidden = (summed * chan_scale[None, :] + residual.astype(jnp.float32)).astype(jnp.bfloat16)
    wide = lax.optimization_barrier(hidden).astype(jnp.float32)
    row_total = lax.psum(jnp.sum(wide * wide, axis=-1), "tp")
    normed = (wide * lax.rsqrt(row_total / DW + 1e-05)[:, None] * norm_gain[None, :]).astype(
        jnp.bfloat16
    )
    block_tables = jnp.take(block_table, mig_request, axis=0)
    counts = jnp.take(cache_blocks, mig_request, axis=0)
    live = jnp.arange(MAX_BLOCK_COUNT, dtype=jnp.int32)[None, :] < counts[:, None]
    send_key = outgoing_blocks(key_pool, block_tables, live)
    send_value = outgoing_blocks(value_block_pool, block_tables, live)
    slot_ids = jnp.arange(MIGS, dtype=jnp.int32)
    me_index = lax.axis_index("replica")
    me_float = me_index.astype(jnp.float32)
    meta = jnp.stack([mig_dest.astype(jnp.float32), counts.astype(jnp.float32)], axis=1).astype(
        jnp.bfloat16
    )
    piece_key = lax.all_gather(send_key, "replica", axis=0, tiled=True)
    piece_value = lax.all_gather(send_value, "replica", axis=0, tiled=True)
    piece_meta = lax.all_gather(meta, "replica", axis=0, tiled=True)
    row_ids = jnp.arange(piece_key.shape[0], dtype=jnp.int32)
    mine = piece_meta[:, 0].astype(jnp.float32) == me_float
    match = mine[None, :] & ((row_ids % MIGS)[None, :] == slot_ids[:, None])
    select = match.astype(jnp.bfloat16)
    add_key = jnp.dot(select, piece_key, preferred_element_type=jnp.float32).astype(jnp.bfloat16)
    add_value = jnp.dot(select, piece_value, preferred_element_type=jnp.float32).astype(
        jnp.bfloat16
    )
    details = jnp.stack(
        [piece_meta[:, 1].astype(jnp.float32), (row_ids // MIGS).astype(jnp.float32)], axis=1
    )
    add_info = jnp.dot(match.astype(jnp.float32), details, precision=lax.Precision.HIGHEST)
    recv_count = add_info[:, 0].astype(jnp.int32)
    recv_source = add_info[:, 1].astype(jnp.int32)
    block_shape = (MIGS, MAX_BLOCK_COUNT) + key_pool.shape[1:]
    recv_key = add_key.reshape(block_shape)
    recv_value = add_value.reshape(block_shape)
    return (hidden, normed, recv_key, recv_value, recv_count, recv_source)


def solution(mesh):
    return jax.shard_map(
        shards,
        mesh=mesh,
        in_specs=(
            P("replica", "tp", None),
            P("replica", "tp", None),
            P("replica", "tp", None),
            P("replica", "tp", None, None),
            P("replica", "tp", None, None),
            P("replica", None),
            P("replica"),
            P("replica"),
            P("replica"),
            P("tp", None),
            P("tp"),
            P("replica", "tp"),
            P("tp"),
        ),
        out_specs=(
            P("replica", "tp"),
            P("replica", "tp"),
            P("replica", None, "tp", None, None),
            P("replica", None, "tp", None, None),
            P("replica"),
            P("replica"),
        ),
        check_vma=False,
    )
```

profile of v0, /device:TPU:1, one launch (start us, length us, event | category | flops | bytes accessed | tf_op | source)
XLA Modules:
  0.0 263.1 jit_solution(17150131231007585839)
XLA Ops:
  8.1 0.9 copy.31
  9.1 0.7 broadcast_multiply_fusion
  9.9 0.7 bitcast_convert_fusion
  10.6 0.6 gather_fusion.3
  11.2 1.5 gather_fusion.2
  12.7 0.8 fusion.16
  13.7 0.9 fusion.24
  15.0 2.9 %convolution_convert_fusion.2 = bf16[4,4096]{1,0:T(4,128)(2,1)S(1)} fusion(bf16[512,4096]{1,0:T(8,128)(2,1)} %param.26, bf16[1,4,4,128]{3,2,1,0:T(4,128)(2,1)S(1)} %fusion.5), kind=kOutput, calls=%fused_computation.8 | convolution fusion | flops 16793600 | bytes 4231168 | tf_op jit(solution)/shard_map/dot_general | solution.py:88
  17.9 1.4 copy.40
  19.9 0.6 gather_fusion
  20.8 0.6 gather_fusion.5
  22.4 1.0 select_bitcast_fusion
  24.2 91.9 %all-gather = bf16[64,2,2]{2,1,0:T(2,128)(2,1)S(1)} all-gather(bf16[1,2,2]{2,1,0:T(2,128)(2,1)S(1)} %bitcast.91), channel_id=1, replica_groups=mesh['replica'=64,'tp'=8] {'replica'}, dimensions={0}, use_global_device_ids=true | all-gather | bytes 520 | tf_op jit(solution)/shard_map/all_gather | solution.py:111
  116.5 1.0 copy.41
  117.7 0.7 convert_reduce_fusion
  118.4 15.3 %psum.7 = f32[4]{0:T(128)S(1)} all-reduce(f32[4]{0:T(128)S(1)} %fusion.7), channel_id=1, replica_groups=mesh['replica'=64,'tp'=8] {'tp'}, use_global_device_ids=true, to_apply=%region_4.6 | all-reduce | flops 4 | bytes 32 | tf_op jit(solution)/shard_map/psum | solution.py:94
  133.7 0.7 fusion.9
  134.4 13.2 %reshape.324 = bf16[128,32768]{1,0:T(8,128)(2,1)} reshape(bf16[64,2,32768]{2,1,0:T(2,128)(2,1)} %all-gather.8.cloned.1.call-done) | data formatting | bytes 16777216
  147.5 4.7 %fusion.1 = bf16[1,2,256,128]{3,1,2,0:T(2,128)(2,1)S(1)} fusion(bf16[128,32768]{1,0:T(8,128)(2,1)} %reshape.324, pred[128]{0:T(512)(128)(4,1)S(1)} %bitcast.89, s32[128]{0:T(128)S(1)} %and_select_fusion.1), kind=kOutput, calls=%fused_computation.10 | convolution fusion | flops 16843264 | bytes 8520320 | tf_op jit(solution)/shard_map/dot_general | solution.py:117
  152.2 0.7 copy.46
  152.9 84.4 %all-gather.6.cloned.1.call-done = bf16[64,2,32768]{2,1,0:T(2,128)(2,1)} async-done(((bf16[1,2,32768]{2,1,0:T(2,128)(2,1)}), bf16[64,2,32768]{2,1,0:T(2,128)(2,1)}) %all-gather.6.cloned.1.call-update) | async-done | bytes 8388624 | tf_op jit(solution)/shard_map/all_gather | solution.py:109
  237.3 13.1 %reshape.322 = bf16[128,32768]{1,0:T(8,128)(2,1)} reshape(bf16[64,2,32768]{2,1,0:T(2,128)(2,1)} %all-gather.6.cloned.1.call-done) | data formatting | bytes 16777216
  250.4 4.6 %fusion = bf16[1,2,256,128]{3,1,2,0:T(2,128)(2,1)S(1)} fusion(bf16[128,32768]{1,0:T(8,128)(2,1)} %reshape.322, pred[128]{0:T(512)(128)(4,1)S(1)} %bitcast.90, s32[128]{0:T(128)S(1)} %and_select_fusion.1), kind=kOutput, calls=%fused_computation.9 | convolution fusion | flops 16843264 | bytes 8520320 | tf_op jit(solution)/shard_map/dot_general | solution.py:116
  255.0 0.7 copy.45
  (66 shorter events, 3.9 us)
Async XLA Ops:
  8.0 2.5 copy-start
  8.0 11.9 %copy-start.1 = (s32[4]{0:T(128)S(1)}, s32[4]{0:T(128)}, u32[]{:S(2)}) copy-start(s32[4]{0:T(128)} %param.23) | copy-start | bytes 52
  8.0 13.3 %copy-start.2 = (bf16[8,1,128,128]{3,2,1,0:T(8,128)(2,1)S(1)}, bf16[8,1,128,128]{3,2,1,0:T(8,128)(2,1)}, u32[]{:S(2)}) copy-start(bf16[8,1,128,128]{3,2,1,0:T(8,128)(2,1)} %param.20) | copy-start | bytes 786436
  8.0 11.3 %copy-start.7 = (s32[2]{0:T(128)S(1)}, s32[2]{0:T(128)}, u32[]{:S(2)}) copy-start(s32[2]{0:T(128)} %param.24) | copy-start | bytes 28
  8.1 16.0 %copy-start.8 = (s32[2]{0:T(128)S(1)}, s32[2]{0:T(128)}, u32[]{:S(2)}) copy-start(s32[2]{0:T(128)} %param.25) | copy-start | bytes 28
  8.1 109.5 %copy-start.4 = (bf16[4,512]{1,0:T(4,128)(2,1)S(1)}, bf16[4,512]{1,0:T(4,128)(2,1)}, u32[]{:S(2)}) copy-start(bf16[4,512]{1,0:T(4,128)(2,1)} %param.28) | copy-start | bytes 12292
  8.1 109.5 %copy-start.5 = (f32[512]{0:T(512)S(1)}, f32[512]{0:T(512)}, u32[]{:S(2)}) copy-start(f32[512]{0:T(512)} %param.27) | copy-start | bytes 6148
  8.1 125.6 %copy-start.6 = (f32[512]{0:T(512)S(1)}, f32[512]{0:T(512)}, u32[]{:S(2)}) copy-start(f32[512]{0:T(512)} %param.29) | copy-start | bytes 6148
  8.1 108.4 %reduce-scatter.4.cloned.1.call-start = ((), (), s32[]{:S(2)}) async-start(), calls=%async_computation.3 | async-start | bytes 1179648
  19.3 115.1 %all-gather.8.cloned.1.call-start = ((), (), s32[]{:S(2)}) async-start(), calls=%async_computation.2 | async-start | bytes 8519680 | tf_op jit(solution)/shard_map/all_gather | solution.py:110
  23.4 213.9 %all-gather.6.cloned.1.call-start = ((), (), s32[]{:S(2)}) async-start(), calls=%async_computation.1 | async-start | bytes 8519680 | tf_op jit(solution)/shard_map/all_gather | solution.py:109
  117.5 30.0 %copy-start.3 = (bf16[4,512]{1,0:T(4,128)(2,1)}, bf16[4,512]{1,0:T(4,128)(2,1)S(1)}, u32[]{:S(2)}) copy-start(bf16[4,512]{1,0:T(4,128)(2,1)S(1)} %add_convert_fusion) | copy-start | bytes 12292
Sparse Core Ops, SparseCore 0:
  19.4 45.9 reduce-scatter.3
Sparse Core Ops, SparseCore 1:
  23.7 110.2 all-gather.7
  137.8 99.5 all-gather.5
where the time goes:
time: 264 us; the launch traced here: 263 us
  blocking collectives  107 us (41%)
  waiting for transfers between devices  85 us (32%)
  local copies, waits for them, and re-layouts  36.3 us (14%)
  between operations  15.7 us (6%)
  matrix products  14.2 us (5%)
  other arithmetic  4.61 us (2%)
    all_gather x1, blocking collectives, shards(): piece_meta = lax.all_gather(meta, 'replica', axis=0, tiled=True)  91.9 us
    all_gather x1, waiting for transfers between devices, shards(): piece_key = lax.all_gather(send_key, 'replica', axis=0, tiled=True)  84.4 us
    unnamed x27, local copies, waits for them, and re-layouts  31.2 us
    psum x1, blocking collectives, shards(): row_total = lax.psum(jnp.sum(wide * wide, axis=-1), 'tp')  15.3 us
  transfers between devices with their start and end apart: 3, of which 1 were waited for; matrix products, arithmetic and copies ran while one was open for 10% of the time, Pallas kernels for 0%

commit v1 on v0

v1 whole, which is shorter than its diff:
```python
import functools
import math

import jax
import jax.numpy as jnp
from jax import lax
from jax.experimental import pallas as pl
from jax.experimental.pallas import tpu as pltpu
from jax.sharding import PartitionSpec as P

MESH = pl.DeviceIdType.MESH
BLOCK = 128
HEAD = 128
ROWS = 512


def body(
    R,
    T,
    bt,
    cb,
    mreq,
    mdest,
    q_ref,
    kn_ref,
    vn_ref,
    kpool_hbm,
    vpool_hbm,
    levels_hbm,
    scale_ref,
    res_ref,
    gain_ref,
    hid_ref,
    norm_ref,
    rk_ref,
    rv_ref,
    cnt_ref,
    src_ref,
    kpool,
    vpool,
    levels,
    q16,
    stage,
    rx1,
    tx2,
    table,
    info_v,
    info_s,
    rs_tx,
    rs_rx,
    ss_tx,
    ss_rx,
    in_sem,
    mig_sem,
    meta_sem,
    info_sem,
    rs_sem,
    ss_sem,
):
    me = lax.axis_index("replica")
    tp = lax.axis_index("tp")
    CR = 2 * ROWS // R
    per_block = BLOCK // CR
    half = R // 2

    copies = [
        pltpu.make_async_copy(kpool_hbm, kpool, in_sem.at[0]),
        pltpu.make_async_copy(vpool_hbm, vpool, in_sem.at[1]),
        pltpu.make_async_copy(levels_hbm, levels, in_sem.at[2]),
    ]
    for c in copies:
        c.start()

    barrier = pltpu.get_barrier_semaphore()

    @pl.loop(1, R)
    def _(i):
        pl.semaphore_signal(
            barrier, inc=1, device_id={"replica": lax.rem(me + i, R)}, device_id_type=MESH
        )

    @pl.loop(1, T)
    def _(i):
        pl.semaphore_signal(
            barrier, inc=1, device_id={"tp": lax.rem(tp + i, T)}, device_id_type=MESH
        )

    lane = lax.broadcasted_iota(jnp.int32, (1, 128), 1)
    r0, r1 = mreq[0], mreq[1]
    c0, c1 = cb[r0], cb[r1]
    row = jnp.where(lane == mdest[0], me * 4 + c0, 0) + jnp.where(
        lane == 64 + mdest[1], me * 4 + c1, 0
    )
    table[me] = row
    copies[0].wait()
    copies[1].wait()
    for j, (r, c) in enumerate(((r0, c0), (r1, c1))):
        for kv, pool in enumerate((kpool, vpool)):
            for b in range(2):
                blk = pool[bt[b, r], 0]
                if b == 1:
                    blk = jnp.where(c > 1, blk, jnp.zeros_like(blk))
                at = (kv * 2 + b) * per_block
                stage[j, at : at + per_block] = blk.reshape(per_block, CR, HEAD)
    my_j = lax.rem(me, 2)
    my_t = me // 2
    rx1[me] = stage[my_j, my_t]

    pl.semaphore_wait(barrier, R + T - 2)

    @pl.loop(1, R)
    def _(i):
        to = lax.rem(me + i, R)
        pltpu.make_async_remote_copy(
            src_ref=table.at[me],
            dst_ref=table.at[me],
            send_sem=meta_sem.at[0],
            recv_sem=meta_sem.at[1],
            device_id={"replica": to},
            device_id_type=MESH,
        ).start()
        pltpu.make_async_remote_copy(
            src_ref=stage.at[lax.rem(to, 2), to // 2],
            dst_ref=rx1.at[me],
            send_sem=mig_sem.at[0],
            recv_sem=mig_sem.at[1],
            device_id={"replica": to},
            device_id_type=MESH,
        ).start()

    for h in range(4):
        for i in range(4):
            q16[4 * h + i : 4 * h + i + 1, :] = q_ref[i, h : h + 1, :].astype(jnp.float32)
    q = q16[...].astype(jnp.bfloat16)
    kn, vn = kn_ref[...], vn_ref[...]
    sm = 1.0 / math.sqrt(HEAD)
    keys = kpool[...].reshape(8 * BLOCK, HEAD)
    dims = (((1,), (1,)), ((), ()))
    scores = lax.dot_general(q, keys, dims, preferred_element_type=jnp.float32) * sm
    own4 = lax.dot_general(q, kn, dims, preferred_element_type=jnp.float32) * sm
    req = lax.rem(lax.broadcasted_iota(jnp.int32, (16, 1), 0), 4)
    first, second = jnp.full((16, 1), -1, jnp.int32), jnp.full((16, 1), -1, jnp.int32)
    for i in range(4):
        first = jnp.where(req == i, bt[0, i], first)
        second = jnp.where(req == i, jnp.where(cb[i] > 1, bt[1, i], -1), second)
    column = lax.broadcasted_iota(jnp.int32, (16, 8 * BLOCK), 1) // BLOCK
    live = (column == first) | (column == second)
    mine = lax.broadcasted_iota(jnp.int32, (16, 4), 1) == req
    own = jnp.sum(jnp.where(mine, own4, 0.0), axis=1, keepdims=True)
    masked = jnp.where(live, scores, jnp.float32(-1e30))
    top = jnp.maximum(jnp.max(masked, axis=1, keepdims=True), own)
    expo = jnp.where(live, jnp.exp(masked - top), 0.0)
    self_expo = jnp.exp(own - top)
    total = jnp.sum(expo, axis=1, keepdims=True) + self_expo
    weights = (expo / total).astype(jnp.bfloat16)
    self_weight = jnp.where(mine, self_expo / total, 0.0).astype(jnp.bfloat16)
    mixed = jnp.dot(
        weights, vpool[...].reshape(8 * BLOCK, HEAD), preferred_element_type=jnp.float32
    ) + jnp.dot(self_weight, vn, preferred_element_type=jnp.float32)
    attn = jnp.concatenate([mixed[4 * h : 4 * h + 4] for h in range(4)], axis=1).astype(
        jnp.bfloat16
    )

    pltpu.make_async_copy(
        table.at[pl.ds(0, R - 1)], table.at[pl.ds(0, R - 1)], meta_sem.at[1]
    ).wait()
    info_v[...] = jnp.sum(table[...], axis=0)
    info_copy = pltpu.make_async_copy(info_v, info_s, info_sem)
    info_copy.start()

    copies[2].wait()
    CW = levels.shape[1] // T

    @pl.loop(0, T)
    def _(i):
        to = lax.rem(tp + 1 + i, T)
        part = jnp.dot(
            attn,
            levels[:, pl.ds(pl.multiple_of(to * CW, CW), CW)],
            preferred_element_type=jnp.float32,
        )
        piece = jnp.concatenate(
            [part[:, 128 * k : 128 * k + 128] for k in range(CW // 128)], axis=0
        )
        rs_tx[to] = piece.astype(jnp.bfloat16)

        @pl.when(i < T - 1)
        def _():
            pltpu.make_async_remote_copy(
                src_ref=rs_tx.at[to],
                dst_ref=rs_rx.at[tp],
                send_sem=rs_sem.at[0],
                recv_sem=rs_sem.at[1],
                device_id={"tp": to},
                device_id_type=MESH,
            ).start()

    rs_rx[tp] = rs_tx[tp]

    info_copy.wait()
    pltpu.make_async_copy(
        rx1.at[pl.ds(0, R - 1)], rx1.at[pl.ds(0, R - 1)], mig_sem.at[1]
    ).wait()
    my_b = lax.rem(my_t // per_block, 2)
    my_k = lax.rem(my_t, per_block)

    def deliver(out):
        @pl.loop(1, R)
        def _(i):
            to = lax.rem(me + i, R)
            tx2[to] = rx1[lax.rem(info_s[0, 64 * my_j + to] // 4, R)]
            pltpu.make_async_remote_copy(
                src_ref=tx2.at[to],
                dst_ref=out.at[my_j, my_b, 0, my_k],
                send_sem=mig_sem.at[2],
                recv_sem=mig_sem.at[3],
                device_id={"replica": to},
                device_id_type=MESH,
            ).start()

        out[my_j, my_b, 0, my_k] = rx1[lax.rem(info_s[0, 64 * my_j + me] // 4, R)]

    @pl.when(my_t < half // 2)
    def _():
        deliver(rk_ref)

    @pl.when(my_t >= half // 2)
    def _():
        deliver(rv_ref)

    for j in range(2):
        word = info_s[0, 64 * j + me]
        src_ref[j] = word // 4
        cnt_ref[j] = lax.rem(word, 4)

    pltpu.make_async_copy(
        rs_rx.at[pl.ds(0, T - 1)], rs_rx.at[pl.ds(0, T - 1)], rs_sem.at[1]
    ).wait()
    sixteen = jnp.sum(rs_rx[...].astype(jnp.float32), axis=0)
    summed = jnp.concatenate([sixteen[4 * k : 4 * k + 4] for k in range(CW // 128)], axis=1)
    hidden = (summed * scale_ref[...] + res_ref[...].astype(jnp.float32)).astype(jnp.bfloat16)
    hid_ref[...] = hidden
    wide = hidden.astype(jnp.float32)
    square = jnp.sum(wide * wide, axis=1, keepdims=True)
    ss_tx[...] = jnp.broadcast_to(square, (4, 128))
    ss_rx[tp] = ss_tx[...]

    @pl.loop(1, T)
    def _(i):
        pltpu.make_async_remote_copy(
            src_ref=ss_tx,
            dst_ref=ss_rx.at[tp],
            send_sem=ss_sem.at[0],
            recv_sem=ss_sem.at[1],
            device_id={"tp": lax.rem(tp + i, T)},
            device_id_type=MESH,
        ).start()

    pltpu.make_async_copy(
        ss_rx.at[pl.ds(0, T - 1)], ss_rx.at[pl.ds(0, T - 1)], ss_sem.at[1]
    ).wait()
    mean = jnp.sum(ss_rx[...], axis=0)[:, 0:1] / (CW * T)
    norm_ref[...] = (wide * lax.rsqrt(mean + 1e-5) * gain_ref[...]).astype(jnp.bfloat16)

    @pl.when(my_j >= 0)
    def _():
        for buf, count, sem in (
            (rx1, R - 1, mig_sem.at[0]),
            (rx1, R - 1, mig_sem.at[2]),
            (rx1, R - 1, mig_sem.at[3]),
            (table, R - 1, meta_sem.at[0]),
            (rs_tx, T - 1, rs_sem.at[0]),
            (ss_rx, T - 1, ss_sem.at[0]),
        ):
            pltpu.make_async_copy(buf.at[pl.ds(0, count)], buf.at[pl.ds(0, count)], sem).wait()


def solution(mesh):
    R, T = mesh.shape["replica"], mesh.shape["tp"]
    CR = 2 * ROWS // R
    per_block = BLOCK // CR

    def shards(q, kn, vn, kpool, vpool, bt, cb, mreq, mdest, levels, scale, res, gain):
        CW = levels.shape[1] // T
        vmem = pl.BlockSpec(memory_space=pltpu.VMEM)
        smem = pl.BlockSpec(memory_space=pltpu.SMEM)
        anyspace = pl.BlockSpec(memory_space=pl.ANY)
        moved = (2, 2, 1, per_block, CR, HEAD)
        bf16, f32, i32 = jnp.bfloat16, jnp.float32, jnp.int32
        hid, norm, rk, rv, cnt, src = pl.pallas_call(
            functools.partial(body, R, T),
            out_shape=(
                jax.ShapeDtypeStruct((4, CW), bf16),
                jax.ShapeDtypeStruct((4, CW), bf16),
                jax.ShapeDtypeStruct(moved, bf16),
                jax.ShapeDtypeStruct(moved, bf16),
                jax.ShapeDtypeStruct((2,), i32),
                jax.ShapeDtypeStruct((2,), i32),
            ),
            in_specs=[smem] * 4 + [vmem] * 3 + [anyspace] * 3 + [vmem] * 3,
            out_specs=(vmem, vmem, vmem, vmem, smem, smem),
            scratch_shapes=[
                pltpu.VMEM((8, 1, BLOCK, HEAD), bf16),
                pltpu.VMEM((8, 1, BLOCK, HEAD), bf16),
                pltpu.VMEM(levels.shape, bf16),
                pltpu.VMEM((16, HEAD), f32),
                pltpu.VMEM((2, R // 2, CR, HEAD), bf16),
                pltpu.VMEM((R, CR, HEAD), bf16),
                pltpu.VMEM((R, CR, HEAD), bf16),
                pltpu.VMEM((R, 1, 128), i32),
                pltpu.VMEM((1, 128), i32),
                pltpu.SMEM((1, 128), i32),
                pltpu.VMEM((T, 4 * CW // 128, 128), bf16),
                pltpu.VMEM((T, 4 * CW // 128, 128), bf16),
                pltpu.VMEM((4, 128), f32),
                pltpu.VMEM((T, 4, 128), f32),
                pltpu.SemaphoreType.DMA((3,)),
                pltpu.SemaphoreType.DMA((4,)),
                pltpu.SemaphoreType.DMA((2,)),
                pltpu.SemaphoreType.DMA,
                pltpu.SemaphoreType.DMA((2,)),
                pltpu.SemaphoreType.DMA((2,)),
            ],
            compiler_params=pltpu.CompilerParams(
                collective_id=0, has_side_effects=True, vmem_limit_bytes=48 * 1024 * 1024
            ),
            name="decode_and_migrate",
        )(
            bt.T,
            cb,
            mreq,
            mdest,
            q,
            kn.reshape(4, HEAD),
            vn.reshape(4, HEAD),
            kpool,
            vpool,
            levels,
            scale[None, :],
            res,
            gain[None, :],
        )
        shape = (2, 2, 1, BLOCK, HEAD)
        return hid, norm, rk.reshape(shape), rv.reshape(shape), cnt, src

    return jax.shard_map(
        shards,
        mesh=mesh,
        in_specs=(
            P("replica", "tp", None),
            P("replica", "tp", None),
            P("replica", "tp", None),
            P("replica", "tp", None, None),
            P("replica", "tp", None, None),
            P("replica", None),
            P("replica"),
            P("replica"),
            P("replica"),
            P("tp", None),
            P("tp"),
            P("replica", "tp"),
            P("tp"),
        ),
        out_specs=(
            P("replica", "tp"),
            P("replica", "tp"),
            P("replica", None, "tp", None, None),
            P("replica", None, "tp", None, None),
            P("replica"),
            P("replica"),
        ),
        check_vma=False,
    )
```

time: 264 us -> 56.6 us (0.21)
  blocking collectives: 107 us -> 0 us
  waiting for transfers between devices: 85 us -> 0 us
  Pallas kernels: 0 us -> 41.1 us
  local copies, waits for them, and re-layouts: 36.3 us -> 14.3 us
  between operations: 15.7 us -> 0.67 us
  matrix products: 14.2 us -> 0 us
  other arithmetic: 4.61 us -> 0 us
    all_gather x1 -> x0, blocking collectives: 91.9 us -> none  [shards(): piece_meta = lax.all_gather(meta, 'replica', axis=0, tiled=True)]
    all_gather x2 -> x0, waiting for transfers between devices: 84.4 us -> none  [the longest x1 84.4 us: shards(): piece_key = lax.all_gather(send_key, 'replica', axis=0, tiled=True)]
    pallas_call x0 -> x1, Pallas kernels: none -> 41.1 us  [shards(): pl.pallas_call(functools.partial(body, R, T), out_shape=(jax.ShapeDtypeSt...]
    unnamed x27 -> x32, local copies, waits for them, and re-layouts: 31.2 us -> 14.3 us
    psum x1 -> x0, blocking collectives: 15.3 us -> none  [shards(): row_total = lax.psum(jnp.sum(wide * wide, axis=-1), 'tp')]
    dot_general x7 -> x0, matrix products: 14.2 us -> none  [the longest x1 4.67 us: shards(): jnp.dot(select, piece_value, preferred_element_type=jnp.float32)]
    gather x6 -> x0, local copies, waits for them, and re-layouts: 4.49 us -> none  [the longest x2 2.15 us: cached_blocks(): picked_blocks = jnp.take(block_pool, block_table.reshape(-1), axis=0)]
  transfers between devices with their start and end apart: 3 -> 0, of which waited for: 1 -> 0; matrix products, arithmetic and copies ran while one was open for 10% -> 0% of each run, Pallas kernels for 0% -> 0%
where the time goes in v1:
time: 56.6 us; the launch traced here: 56.1 us
  Pallas kernels  41.1 us (73%)
  local copies, waits for them, and re-layouts  14.3 us (25%)
  between operations  0.67 us (1%)
    pallas_call x1, Pallas kernels, shards(): pl.pallas_call(functools.partial(body, R, T), out_shape=(jax.ShapeDtypeSt...  41.1 us
    unnamed x32, local copies, waits for them, and re-layouts  14.3 us

profile of v1, /device:TPU:1, one launch (start us, length us, event | category | flops | bytes accessed | tf_op | source)
XLA Modules:
  0.0 56.1 jit_solution(16037014738371164355)
XLA Ops:
  0.6 0.0 copy-start
  0.6 2.2 %copy-done = bf16[512,4096]{1,0:T(8,128)(2,1)S(1)} copy-done((bf16[512,4096]{1,0:T(8,128)(2,1)S(1)}, bf16[512,4096]{1,0:T(8,128)(2,1)}, u32[]{:S(2)}) %copy-start) | copy-done | bytes 4194328
  2.8 0.0 copy-start.1
  2.8 0.9 %copy-done.1 = bf16[8,1,128,128]{3,2,1,0:T(8,128)(2,1)S(1)} copy-done((bf16[8,1,128,128]{3,2,1,0:T(8,128)(2,1)S(1)}, bf16[8,1,128,128]{3,2,1,0:T(8,128)(2,1)}, u32[]{:S(2)}) %copy-start.1) | copy-done | bytes 262168
  3.8 0.0 copy-start.2
  3.8 0.9 %copy-done.2 = bf16[8,1,128,128]{3,2,1,0:T(8,128)(2,1)S(1)} copy-done((bf16[8,1,128,128]{3,2,1,0:T(8,128)(2,1)S(1)}, bf16[8,1,128,128]{3,2,1,0:T(8,128)(2,1)}, u32[]{:S(2)}) %copy-start.2) | copy-done | bytes 262168
  4.7 0.0 copy-start.3
  4.7 0.7 %copy-done.3 = bf16[4,4,128]{2,1,0:T(4,128)(2,1)S(1)} copy-done((bf16[4,4,128]{2,1,0:T(4,128)(2,1)S(1)}, bf16[4,4,128]{2,1,0:T(4,128)(2,1)}, u32[]{:S(2)}) %copy-start.3) | copy-done | bytes 4120
  5.4 0.7 %copy-done.4 = bf16[4,512]{1,0:T(4,128)(2,1)S(1)} copy-done((bf16[4,512]{1,0:T(4,128)(2,1)S(1)}, bf16[4,512]{1,0:T(4,128)(2,1)}, u32[]{:S(2)}) %copy-start.4) | copy-done | bytes 4120
  6.1 0.7 %copy-done.5 = f32[512]{0:T(512)S(1)} copy-done((f32[512]{0:T(512)S(1)}, f32[512]{0:T(512)}, u32[]{:S(2)}) %copy-start.5) | copy-done | bytes 2072
  6.8 0.7 %copy-done.6 = f32[512]{0:T(512)S(1)} copy-done((f32[512]{0:T(512)S(1)}, f32[512]{0:T(512)}, u32[]{:S(2)}) %copy-start.6) | copy-done | bytes 2072
  7.5 0.7 %copy-done.7 = s32[4,2]{0,1:T(2,128)S(1)} copy-done((s32[4,2]{0,1:T(2,128)S(1)}, s32[4,2]{0,1:T(2,128)}, u32[]{:S(2)}) %copy-start.7) | copy-done | bytes 56
  8.1 0.7 %copy-done.8 = bf16[4,1,128]{2,0,1:T(4,128)(2,1)S(1)} copy-done((bf16[4,1,128]{2,0,1:T(4,128)(2,1)S(1)}, bf16[4,1,128]{2,0,1:T(4,128)(2,1)}, u32[]{:S(2)}) %copy-start.8) | copy-done | bytes 1048
  8.8 0.7 %copy-done.9 = bf16[4,1,128]{2,0,1:T(4,128)(2,1)S(1)} copy-done((bf16[4,1,128]{2,0,1:T(4,128)(2,1)S(1)}, bf16[4,1,128]{2,0,1:T(4,128)(2,1)}, u32[]{:S(2)}) %copy-start.9) | copy-done | bytes 1048
  9.5 0.7 %copy-done.10 = s32[4]{0:T(128)S(1)} copy-done((s32[4]{0:T(128)S(1)}, s32[4]{0:T(128)}, u32[]{:S(2)}) %copy-start.10) | copy-done | bytes 40
  10.2 0.7 %copy-done.11 = s32[2]{0:T(128)S(1)} copy-done((s32[2]{0:T(128)S(1)}, s32[2]{0:T(128)}, u32[]{:S(2)}) %copy-start.11) | copy-done | bytes 32
  10.8 0.7 %copy-done.12 = s32[2]{0:T(128)S(1)} copy-done((s32[2]{0:T(128)S(1)}, s32[2]{0:T(128)}, u32[]{:S(2)}) %copy-start.12) | copy-done | bytes 32
  11.5 41.1 %decode_and_migrate.1 = (bf16[4,512]{1,0:T(4,128)(2,1)S(1)}, bf16[4,512]{1,0:T(4,128)(2,1)S(1)}, bf16[2,2,1,8,16,128]{5,4,3,2,1,0:T(8,128)(2,1)S(1)}, bf16[2,2,1...) custom-call(s32[2,4]{1,0:T(2,128)S(1)} %bitcast.15, s32[4]{0:T(128)S(1)} %copy-done.10, ...), custom_call_target="tpu_custom_call" | custom-call | tf_op jit(solution)/shard_map/decode_and_migrate/pallas_call | solution.py:290
  52.6 0.6 %copy.27 = bf16[4,512]{1,0:T(4,128)(2,1)} copy(bf16[4,512]{1,0:T(4,128)(2,1)S(1)} %get-tuple-element.30) | data formatting | bytes 8192
  53.2 0.6 %copy.28 = bf16[4,512]{1,0:T(4,128)(2,1)} copy(bf16[4,512]{1,0:T(4,128)(2,1)S(1)} %get-tuple-element.31) | data formatting | bytes 8192
  53.8 0.7 %copy.29 = bf16[2,2,1,128,128]{4,3,2,1,0:T(8,128)(2,1)} copy(bf16[2,2,1,128,128]{4,3,2,1,0:T(8,128)(2,1)S(1)} %bitcast.12) | data formatting | bytes 262144
  54.5 0.7 %copy.30 = bf16[2,2,1,128,128]{4,3,2,1,0:T(8,128)(2,1)} copy(bf16[2,2,1,128,128]{4,3,2,1,0:T(8,128)(2,1)S(1)} %bitcast.11) | data formatting | bytes 262144
  55.1 0.5 copy.31
  55.6 0.5 copy.32
  (9 shorter events, 0.0 us)
Async XLA Ops:
  0.6 2.2 %copy-start = (bf16[512,4096]{1,0:T(8,128)(2,1)S(1)}, bf16[512,4096]{1,0:T(8,128)(2,1)}, u32[]{:S(2)}) copy-start(bf16[512,4096]{1,0:T(8,128)(2,1)} %levels_hbm.1) | copy-start | bytes 12582916
  2.8 0.9 %copy-start.1 = (bf16[8,1,128,128]{3,2,1,0:T(8,128)(2,1)S(1)}, bf16[8,1,128,128]{3,2,1,0:T(8,128)(2,1)}, u32[]{:S(2)}) copy-start(bf16[8,1,128,128]{3,2,1,0:T(8,128)(2,1)} %kpool_hbm.1) | copy-start | bytes 786436
  3.8 0.9 %copy-start.2 = (bf16[8,1,128,128]{3,2,1,0:T(8,128)(2,1)S(1)}, bf16[8,1,128,128]{3,2,1,0:T(8,128)(2,1)}, u32[]{:S(2)}) copy-start(bf16[8,1,128,128]{3,2,1,0:T(8,128)(2,1)} %vpool_hbm.1) | copy-start | bytes 786436
  4.7 0.7 %copy-start.3 = (bf16[4,4,128]{2,1,0:T(4,128)(2,1)S(1)}, bf16[4,4,128]{2,1,0:T(4,128)(2,1)}, u32[]{:S(2)}) copy-start(bf16[4,4,128]{2,1,0:T(4,128)(2,1)} %q_ref.1) | copy-start | bytes 12292
  5.4 0.7 %copy-start.4 = (bf16[4,512]{1,0:T(4,128)(2,1)S(1)}, bf16[4,512]{1,0:T(4,128)(2,1)}, u32[]{:S(2)}) copy-start(bf16[4,512]{1,0:T(4,128)(2,1)} %res_ref.1) | copy-start | bytes 12292
  6.1 0.7 %copy-start.5 = (f32[512]{0:T(512)S(1)}, f32[512]{0:T(512)}, u32[]{:S(2)}) copy-start(f32[512]{0:T(512)} %param.23) | copy-start | bytes 6148
  6.8 0.7 %copy-start.6 = (f32[512]{0:T(512)S(1)}, f32[512]{0:T(512)}, u32[]{:S(2)}) copy-start(f32[512]{0:T(512)} %param.25) | copy-start | bytes 6148
  7.5 0.7 %copy-start.7 = (s32[4,2]{0,1:T(2,128)S(1)}, s32[4,2]{0,1:T(2,128)}, u32[]{:S(2)}) copy-start(s32[4,2]{0,1:T(2,128)} %param.18) | copy-start | bytes 100
  8.1 0.7 %copy-start.8 = (bf16[4,1,128]{2,0,1:T(4,128)(2,1)S(1)}, bf16[4,1,128]{2,0,1:T(4,128)(2,1)}, u32[]{:S(2)}) copy-start(bf16[4,1,128]{2,0,1:T(4,128)(2,1)} %param.14) | copy-start | bytes 3076
  8.8 0.7 %copy-start.9 = (bf16[4,1,128]{2,0,1:T(4,128)(2,1)S(1)}, bf16[4,1,128]{2,0,1:T(4,128)(2,1)}, u32[]{:S(2)}) copy-start(bf16[4,1,128]{2,0,1:T(4,128)(2,1)} %param.15) | copy-start | bytes 3076
  9.5 0.7 %copy-start.10 = (s32[4]{0:T(128)S(1)}, s32[4]{0:T(128)}, u32[]{:S(2)}) copy-start(s32[4]{0:T(128)} %cb.1) | copy-start | bytes 52
  10.2 0.7 %copy-start.11 = (s32[2]{0:T(128)S(1)}, s32[2]{0:T(128)}, u32[]{:S(2)}) copy-start(s32[2]{0:T(128)} %mreq.1) | copy-start | bytes 28
  10.8 0.7 %copy-start.12 = (s32[2]{0:T(128)S(1)}, s32[2]{0:T(128)}, u32[]{:S(2)}) copy-start(s32[2]{0:T(128)} %mdest.1) | copy-start | bytes 28

commit v2 on v1

--- a/solution.py
+++ b/solution.py
@@ -17,28 +17,42 @@
 def body(
     R,
     T,
+    bt_hbm,
+    cb_hbm,
+    mreq_hbm,
+    mdest_hbm,
+    kpool_hbm,
+    vpool_hbm,
+    q_hbm,
+    kn_hbm,
+    vn_hbm,
+    levels_hbm,
+    scale_hbm,
+    res_hbm,
+    gain_hbm,
+    hid_out,
+    norm_out,
+    rk_ref,
+    rv_ref,
+    cnt_out,
+    src_out,
     bt,
     cb,
     mreq,
     mdest,
+    kpool,
+    vpool,
     q_ref,
     kn_ref,
     vn_ref,
-    kpool_hbm,
-    vpool_hbm,
-    levels_hbm,
+    levels,
     scale_ref,
     res_ref,
     gain_ref,
+    cnt_ref,
+    src_ref,
     hid_ref,
     norm_ref,
-    rk_ref,
-    rv_ref,
-    cnt_ref,
-    src_ref,
-    kpool,
-    vpool,
-    levels,
     q16,
     stage,
     rx1,
@@ -56,6 +70,7 @@
     info_sem,
     rs_sem,
     ss_sem,
+    out_sem,
 ):
     me = lax.axis_index("replica")
     tp = lax.axis_index("tp")
@@ -64,11 +79,26 @@
     half = R // 2
 
     copies = [
-        pltpu.make_async_copy(kpool_hbm, kpool, in_sem.at[0]),
-        pltpu.make_async_copy(vpool_hbm, vpool, in_sem.at[1]),
-        pltpu.make_async_copy(levels_hbm, levels, in_sem.at[2]),
+        pltpu.make_async_copy(src, dst, in_sem.at[n])
+        for n, (src, dst) in enumerate(
+            (
+                (bt_hbm, bt),
+                (cb_hbm, cb),
+                (mreq_hbm, mreq),
+                (mdest_hbm, mdest),
+                (kpool_hbm, kpool),
+                (vpool_hbm, vpool),
+                (q_hbm, q_ref),
+                (kn_hbm, kn_ref),
+                (vn_hbm, vn_ref),
+                (levels_hbm, levels),
+                (scale_hbm, scale_ref),
+                (res_hbm, res_ref),
+                (gain_hbm, gain_ref),
+            )
+        )
     ]
-    for c in copies:
+    for c in copies[:6]:
         c.start()
 
     barrier = pltpu.get_barrier_semaphore()
@@ -84,6 +114,11 @@
         pl.semaphore_signal(
             barrier, inc=1, device_id={"tp": lax.rem(tp + i, T)}, device_id_type=MESH
         )
+
+    for c in copies[6:]:
+        c.start()
+    for c in copies[:4]:
+        c.wait()
 
     lane = lax.broadcasted_iota(jnp.int32, (1, 128), 1)
     r0, r1 = mreq[0], mreq[1]
@@ -92,8 +127,8 @@
         lane == 64 + mdest[1], me * 4 + c1, 0
     )
     table[me] = row
-    copies[0].wait()
-    copies[1].wait()
+    copies[4].wait()
+    copies[5].wait()
     for j, (r, c) in enumerate(((r0, c0), (r1, c1))):
         for kv, pool in enumerate((kpool, vpool)):
             for b in range(2):
@@ -127,6 +162,9 @@
             device_id={"replica": to},
             device_id_type=MESH,
         ).start()
+
+    for c in copies[6:9]:
+        c.wait()
 
     for h in range(4):
         for i in range(4):
@@ -168,7 +206,7 @@
     info_copy = pltpu.make_async_copy(info_v, info_s, info_sem)
     info_copy.start()
 
-    copies[2].wait()
+    copies[9].wait()
     CW = levels.shape[1] // T
 
     @pl.loop(0, T)
@@ -218,7 +256,8 @@
                 device_id_type=MESH,
             ).start()
 
-        out[my_j, my_b, 0, my_k] = rx1[lax.rem(info_s[0, 64 * my_j + me] // 4, R)]
+        tx2[me] = rx1[lax.rem(info_s[0, 64 * my_j + me] // 4, R)]
+        pltpu.make_async_copy(tx2.at[me], out.at[my_j, my_b, 0, my_k], out_sem.at[4]).start()
 
     @pl.when(my_t < half // 2)
     def _():
@@ -232,6 +271,14 @@
         word = info_s[0, 64 * j + me]
         src_ref[j] = word // 4
         cnt_ref[j] = lax.rem(word, 4)
+    small = [
+        pltpu.make_async_copy(cnt_ref, cnt_out, out_sem.at[0]),
+        pltpu.make_async_copy(src_ref, src_out, out_sem.at[1]),
+    ]
+    for c in small:
+        c.start()
+    for c in copies[10:]:
+        c.wait()
 
     pltpu.make_async_copy(
         rs_rx.at[pl.ds(0, T - 1)], rs_rx.at[pl.ds(0, T - 1)], rs_sem.at[1]
@@ -240,6 +287,8 @@
     summed = jnp.concatenate([sixteen[4 * k : 4 * k + 4] for k in range(CW // 128)], axis=1)
     hidden = (summed * scale_ref[...] + res_ref[...].astype(jnp.float32)).astype(jnp.bfloat16)
     hid_ref[...] = hidden
+    small.append(pltpu.make_async_copy(hid_ref, hid_out, out_sem.at[2]))
+    small[-1].start()
     wide = hidden.astype(jnp.float32)
     square = jnp.sum(wide * wide, axis=1, keepdims=True)
     ss_tx[...] = jnp.broadcast_to(square, (4, 128))
@@ -262,17 +311,34 @@
     mean = jnp.sum(ss_rx[...], axis=0)[:, 0:1] / (CW * T)
     norm_ref[...] = (wide * lax.rsqrt(mean + 1e-5) * gain_ref[...]).astype(jnp.bfloat16)
 
-    @pl.when(my_j >= 0)
-    def _():
-        for buf, count, sem in (
-            (rx1, R - 1, mig_sem.at[0]),
-            (rx1, R - 1, mig_sem.at[2]),
-            (rx1, R - 1, mig_sem.at[3]),
-            (table, R - 1, meta_sem.at[0]),
-            (rs_tx, T - 1, rs_sem.at[0]),
-            (ss_rx, T - 1, ss_sem.at[0]),
-        ):
-            pltpu.make_async_copy(buf.at[pl.ds(0, count)], buf.at[pl.ds(0, count)], sem).wait()
+    small.append(pltpu.make_async_copy(norm_ref, norm_out, out_sem.at[3]))
+    small[-1].start()
+
+    for c in small:
+        c.wait()
+    pltpu.make_async_copy(tx2.at[0], rk_ref.at[0, 0, 0, 0], out_sem.at[4]).wait()
+    for buf, count, sem in (
+        (rx1, R - 1, mig_sem.at[0]),
+        (rx1, R - 1, mig_sem.at[2]),
+        (rx1, R - 1, mig_sem.at[3]),
+        (table, R - 1, meta_sem.at[0]),
+        (rs_tx, T - 1, rs_sem.at[0]),
+        (ss_rx, T - 1, ss_sem.at[0]),
+    ):
+        pltpu.make_async_copy(buf.at[pl.ds(0, count)], buf.at[pl.ds(0, count)], sem).wait()
+
+
+def emit(n, *refs):
+    ins, outs, held, sem = refs[:n], refs[n : 2 * n], refs[2 * n : 3 * n], refs[3 * n]
+    loads = [pltpu.make_async_copy(ins[i], held[i], sem.at[0, i]) for i in range(n)]
+    stores = [pltpu.make_async_copy(held[i], outs[i], sem.at[1, i]) for i in range(n)]
+    for c in loads:
+        c.start()
+    for c, d in zip(loads, stores):
+        c.wait()
+        d.start()
+    for c in stores:
+        c.wait()
 
 
 def solution(mesh):
@@ -283,11 +349,10 @@
     def shards(q, kn, vn, kpool, vpool, bt, cb, mreq, mdest, levels, scale, res, gain):
         CW = levels.shape[1] // T
         vmem = pl.BlockSpec(memory_space=pltpu.VMEM)
-        smem = pl.BlockSpec(memory_space=pltpu.SMEM)
-        anyspace = pl.BlockSpec(memory_space=pl.ANY)
+        hbm = pl.BlockSpec(memory_space=pltpu.HBM)
         moved = (2, 2, 1, per_block, CR, HEAD)
         bf16, f32, i32 = jnp.bfloat16, jnp.float32, jnp.int32
-        hid, norm, rk, rv, cnt, src = pl.pallas_call(
+        results = pl.pallas_call(
             functools.partial(body, R, T),
             out_shape=(
                 jax.ShapeDtypeStruct((4, CW), bf16),
@@ -297,12 +362,26 @@
                 jax.ShapeDtypeStruct((2,), i32),
                 jax.ShapeDtypeStruct((2,), i32),
             ),
-            in_specs=[smem] * 4 + [vmem] * 3 + [anyspace] * 3 + [vmem] * 3,
-            out_specs=(vmem, vmem, vmem, vmem, smem, smem),
+            in_specs=[hbm] * 13,
+            out_specs=(hbm,) * 6,
             scratch_shapes=[
+                pltpu.SMEM((2, 4), i32),
+                pltpu.SMEM((4,), i32),
+                pltpu.SMEM((2,), i32),
+                pltpu.SMEM((2,), i32),
                 pltpu.VMEM((8, 1, BLOCK, HEAD), bf16),
                 pltpu.VMEM((8, 1, BLOCK, HEAD), bf16),
+                pltpu.VMEM((4, 4, HEAD), bf16),
+                pltpu.VMEM((4, HEAD), bf16),
+                pltpu.VMEM((4, HEAD), bf16),
                 pltpu.VMEM(levels.shape, bf16),
+                pltpu.VMEM((1, CW), f32),
+                pltpu.VMEM((4, CW), bf16),
+                pltpu.VMEM((1, CW), f32),
+                pltpu.SMEM((2,), i32),
+                pltpu.SMEM((2,), i32),
+                pltpu.VMEM((4, CW), bf16),
+                pltpu.VMEM((4, CW), bf16),
                 pltpu.VMEM((16, HEAD), f32),
                 pltpu.VMEM((2, R // 2, CR, HEAD), bf16),
                 pltpu.VMEM((R, CR, HEAD), bf16),
@@ -314,15 +393,16 @@
                 pltpu.VMEM((T, 4 * CW // 128, 128), bf16),
                 pltpu.VMEM((4, 128), f32),
                 pltpu.VMEM((T, 4, 128), f32),
-                pltpu.SemaphoreType.DMA((3,)),
+                pltpu.SemaphoreType.DMA((13,)),
                 pltpu.SemaphoreType.DMA((4,)),
                 pltpu.SemaphoreType.DMA((2,)),
                 pltpu.SemaphoreType.DMA,
                 pltpu.SemaphoreType.DMA((2,)),
                 pltpu.SemaphoreType.DMA((2,)),
+                pltpu.SemaphoreType.DMA((5,)),
             ],
             compiler_params=pltpu.CompilerParams(
-                collective_id=0, has_side_effects=True, vmem_limit_bytes=48 * 1024 * 1024
+                collective_id=0, has_side_effects=True, vmem_limit_bytes=60 * 1024 * 1024
             ),
             name="decode_and_migrate",
         )(
@@ -330,16 +410,26 @@
             cb,
             mreq,
             mdest,
+            kpool,
+            vpool,
             q,
             kn.reshape(4, HEAD),
             vn.reshape(4, HEAD),
-            kpool,
-            vpool,
             levels,
             scale[None, :],
             res,
             gain[None, :],
         )
+        hid, norm, rk, rv, cnt, src = pl.pallas_call(
+            functools.partial(emit, 6),
+            out_shape=tuple(jax.ShapeDtypeStruct(r.shape, r.dtype) for r in results),
+            in_specs=[hbm] * 6,
+            out_specs=(hbm,) * 6,
+            scratch_shapes=[pltpu.VMEM(r.shape, r.dtype) for r in results]
+            + [pltpu.SemaphoreType.DMA((2, 6))],
+            compiler_params=pltpu.CompilerParams(vmem_limit_bytes=60 * 1024 * 1024),
+            name="write_outputs",
+        )(*results)
         shape = (2, 2, 1, BLOCK, HEAD)
         return hid, norm, rk.reshape(shape), rv.reshape(shape), cnt, src
 

time: 56.6 us -> 42.5 us (0.75)
  local copies, waits for them, and re-layouts: 14.3 us -> 0 us
  Pallas kernels: 41.1 us -> 41.7 us
    unnamed x32 -> x0, local copies, waits for them, and re-layouts: 14.3 us -> none
    pallas_call x0 -> x1, Pallas kernels: none -> 1.74 us  [shards(): pl.pallas_call(functools.partial(emit, 6), out_shape=tuple((jax.ShapeDtyp...]
    pallas_call x1, Pallas kernels: 41.1 us -> 39.9 us  [shards(): pl.pallas_call(functools.partial(body, R, T), out_shape=(jax.ShapeDtypeSt...]
where the time goes in v2:
time: 42.5 us; the launch traced here: 42.3 us
  Pallas kernels  41.7 us (98%)
  between operations  0.65 us (2%)
    pallas_call x1, Pallas kernels, shards(): pl.pallas_call(functools.partial(body, R, T), out_shape=(jax.ShapeDtypeSt...  39.9 us
    pallas_call x1, Pallas kernels, shards(): pl.pallas_call(functools.partial(emit, 6), out_shape=tuple((jax.ShapeDtyp...  1.74 us

profile of v2, /device:TPU:1, one launch (start us, length us, event | category | flops | bytes accessed | tf_op | source)
XLA Modules:
  0.0 42.3 jit_solution(6045501711990580816)
XLA Ops:
  0.6 39.9 %decode_and_migrate.1 = (bf16[4,512]{1,0:T(4,128)(2,1)}, bf16[4,512]{1,0:T(4,128)(2,1)}, bf16[2,2,1,8,16,128]{5,4,3,2,1,0:T(8,128)(2,1)}, bf16[2,2,1,8,16,128]{5...) custom-call(s32[2,4]{1,0:T(2,128)} %bitcast.13, s32[4]{0:T(128)} %cb_hbm.1, s32[2]{0:T(128)} %mreq_hbm.1, s32[2]{0:T(128)} %mdest_hbm.1, ...), custom_call_target="tpu_custom_call" | custom-call | tf_op jit(solution)/shard_map/decode_and_migrate/pallas_call | solution.py:355
  40.6 1.7 %write_outputs.1 = (bf16[4,512]{1,0:T(4,128)(2,1)}, bf16[4,512]{1,0:T(4,128)(2,1)}, bf16[2,2,1,8,16,128]{5,4,3,2,1,0:T(8,128)(2,1)}, bf16[2,2,1,8,16,128]{5,4,3,...) custom-call(bf16[4,512]{1,0:T(4,128)(2,1)} %get-tuple-element.18.refs_0_, bf16[4,512]{1,0:T(4,128)(2,1)} %get-tuple-element.19.refs_1_, ...), custom_call_target="tpu_custom_call" | custom-call | tf_op jit(solution)/shard_map/write_outputs/pallas_call | solution.py:423

commit v3 on v2

--- a/solution.py
+++ b/solution.py
@@ -12,6 +12,14 @@
 BLOCK = 128
 HEAD = 128
 ROWS = 512
+
+
+def outward(centre, i):
+    return jnp.where(lax.rem(i, 2) == 1, centre - (i + 1) // 2, centre + i // 2)
+
+
+def spread(n):
+    return sorted(range(n), key=lambda d: -min(d, n - d))
 
 
 def body(
@@ -77,6 +85,20 @@
     CR = 2 * ROWS // R
     per_block = BLOCK // CR
     half = R // 2
+    X = min(4, T)
+    my_x = lax.rem(tp, X)
+    Z = min(8, R // 2)
+    Y = R // (2 * Z)
+    my_y, my_z, core = me // (2 * Z), lax.rem(me // 2, Z), lax.rem(me, 2)
+
+    ys = [lax.rem(my_y + d, Y) for d in spread(Y)]
+
+    def plane(z):
+        chips = [(y * Z + z) * 2 for y in ys]
+        return [chip + c for chip in chips for c in (1 - core, core)]
+
+    def farthest_first(i):
+        return lax.rem(my_z + outward(Z // 2, i), Z)
 
     copies = [
         pltpu.make_async_copy(src, dst, in_sem.at[n])
@@ -103,11 +125,18 @@
 
     barrier = pltpu.get_barrier_semaphore()
 
-    @pl.loop(1, R)
+    def greet(to):
+        pl.semaphore_signal(barrier, inc=1, device_id={"replica": to}, device_id_type=MESH)
+
+    @pl.loop(0, Z)
     def _(i):
-        pl.semaphore_signal(
-            barrier, inc=1, device_id={"replica": lax.rem(me + i, R)}, device_id_type=MESH
-        )
+        peers = plane(farthest_first(i))
+        for to in peers[:-1]:
+            greet(to)
+
+        @pl.when(i < Z - 1)
+        def _():
+            greet(peers[-1])
 
     @pl.loop(1, T)
     def _(i):
@@ -120,13 +149,13 @@
     for c in copies[:4]:
         c.wait()
 
-    lane = lax.broadcasted_iota(jnp.int32, (1, 128), 1)
+    lane = lax.broadcasted_iota(jnp.int32, (2, 128), 1)
+    kind = lax.broadcasted_iota(jnp.int32, (2, 128), 0)
     r0, r1 = mreq[0], mreq[1]
     c0, c1 = cb[r0], cb[r1]
-    row = jnp.where(lane == mdest[0], me * 4 + c0, 0) + jnp.where(
-        lane == 64 + mdest[1], me * 4 + c1, 0
+    table[me] = jnp.where(lane == mdest[0], jnp.where(kind == 0, me, c0), 0) + jnp.where(
+        lane == 64 + mdest[1], jnp.where(kind == 0, me, c1), 0
     )
-    table[me] = row
     copies[4].wait()
     copies[5].wait()
     for j, (r, c) in enumerate(((r0, c0), (r1, c1))):
@@ -141,19 +170,127 @@
     my_t = me // 2
     rx1[me] = stage[my_j, my_t]
 
+    CW = levels.shape[1] // T
+
+    def compute():
+        for c in copies[6:9]:
+            c.wait()
+
+        for h in range(4):
+            for i in range(4):
+                q16[4 * h + i : 4 * h + i + 1, :] = q_ref[i, h : h + 1, :].astype(jnp.float32)
+        q = q16[...].astype(jnp.bfloat16)
+        kn, vn = kn_ref[...], vn_ref[...]
+        sm = 1.0 / math.sqrt(HEAD)
+        keys = kpool[...].reshape(8 * BLOCK, HEAD)
+        dims = (((1,), (1,)), ((), ()))
+        scores = lax.dot_general(q, keys, dims, preferred_element_type=jnp.float32) * sm
+        own4 = lax.dot_general(q, kn, dims, preferred_element_type=jnp.float32) * sm
+        req = lax.rem(lax.broadcasted_iota(jnp.int32, (16, 1), 0), 4)
+        first, second = jnp.full((16, 1), -1, jnp.int32), jnp.full((16, 1), -1, jnp.int32)
+        for i in range(4):
+            first = jnp.where(req == i, bt[0, i], first)
+            second = jnp.where(req == i, jnp.where(cb[i] > 1, bt[1, i], -1), second)
+        column = lax.broadcasted_iota(jnp.int32, (16, 8 * BLOCK), 1) // BLOCK
+        live = (column == first) | (column == second)
+        mine = lax.broadcasted_iota(jnp.int32, (16, 4), 1) == req
+        own = jnp.sum(jnp.where(mine, own4, 0.0), axis=1, keepdims=True)
+        masked = jnp.where(live, scores, jnp.float32(-1e30))
+        top = jnp.maximum(jnp.max(masked, axis=1, keepdims=True), own)
+        expo = jnp.where(live, jnp.exp(masked - top), 0.0)
+        self_expo = jnp.exp(own - top)
+        total = jnp.sum(expo, axis=1, keepdims=True) + self_expo
+        weights = (expo / total).astype(jnp.bfloat16)
+        self_weight = jnp.where(mine, self_expo / total, 0.0).astype(jnp.bfloat16)
+        mixed = jnp.dot(
+            weights, vpool[...].reshape(8 * BLOCK, HEAD), preferred_element_type=jnp.float32
+        ) + jnp.dot(self_weight, vn, preferred_element_type=jnp.float32)
+        attn = jnp.concatenate([mixed[4 * h : 4 * h + 4] for h in range(4)], axis=1).astype(
+            jnp.bfloat16
+        )
+
+        copies[9].wait()
+
+        @pl.loop(0, T)
+        def _(to):
+            part = jnp.dot(
+                attn,
+                levels[:, pl.ds(pl.multiple_of(to * CW, CW), CW)],
+                preferred_element_type=jnp.float32,
+            )
+            piece = jnp.concatenate(
+                [part[:, 128 * k : 128 * k + 128] for k in range(CW // 128)], axis=0
+            )
+            rs_tx[to] = piece.astype(jnp.bfloat16)
+
+    hid_copy = pltpu.make_async_copy(hid_ref, hid_out, out_sem.at[2])
+
+    def reduce_scatter():
+        rs_rx[tp] = rs_tx[tp]
+
+        @pl.loop(1, T)
+        def _(i):
+            to = lax.rem(tp + i, T)
+            pltpu.make_async_remote_copy(
+                src_ref=rs_tx.at[to],
+                dst_ref=rs_rx.at[tp],
+                send_sem=rs_sem.at[0],
+                recv_sem=rs_sem.at[1],
+                device_id={"tp": to},
+                device_id_type=MESH,
+            ).start()
+
+    def finish_hidden():
+        for c in copies[10:]:
+            c.wait()
+
+        pltpu.make_async_copy(
+            rs_rx.at[pl.ds(0, T - 1)], rs_rx.at[pl.ds(0, T - 1)], rs_sem.at[1]
+        ).wait()
+        sixteen = jnp.sum(rs_rx[...].astype(jnp.float32), axis=0)
+        summed = jnp.concatenate([sixteen[4 * k : 4 * k + 4] for k in range(CW // 128)], axis=1)
+        hidden = (summed * scale_ref[...] + res_ref[...].astype(jnp.float32)).astype(jnp.bfloat16)
+        hid_ref[...] = hidden
+        hid_copy.start()
+        wide = hidden.astype(jnp.float32)
+        square = jnp.sum(wide * wide, axis=1, keepdims=True)
+        ss_tx[...] = jnp.broadcast_to(square, (4, 128))
+        ss_rx[tp] = ss_tx[...]
+
+        @pl.loop(1, T)
+        def _(i):
+            pltpu.make_async_remote_copy(
+                src_ref=ss_tx,
+                dst_ref=ss_rx.at[tp],
+                send_sem=ss_sem.at[0],
+                recv_sem=ss_sem.at[1],
+                device_id={"tp": lax.rem(tp + i, T)},
+                device_id_type=MESH,
+            ).start()
+
+    early = my_z < Z // 2
+    pl.when(early)(compute)
+
     pl.semaphore_wait(barrier, R + T - 2)
 
-    @pl.loop(1, R)
+    pl.when(early)(reduce_scatter)
+
+    @pl.loop(0, R // X)
     def _(i):
-        to = lax.rem(me + i, R)
-        pltpu.make_async_remote_copy(
-            src_ref=table.at[me],
-            dst_ref=table.at[me],
-            send_sem=meta_sem.at[0],
-            recv_sem=meta_sem.at[1],
-            device_id={"replica": to},
-            device_id_type=MESH,
-        ).start()
+        to = i * X + my_x
+
+        @pl.when(to != me)
+        def _():
+            pltpu.make_async_remote_copy(
+                src_ref=table.at[me],
+                dst_ref=table.at[me],
+                send_sem=meta_sem.at[0],
+                recv_sem=meta_sem.at[1],
+                device_id={"replica": to},
+                device_id_type=MESH,
+            ).start()
+
+    def scatter(to):
         pltpu.make_async_remote_copy(
             src_ref=stage.at[lax.rem(to, 2), to // 2],
             dst_ref=rx1.at[me],
@@ -163,77 +300,49 @@
             device_id_type=MESH,
         ).start()
 
-    for c in copies[6:9]:
-        c.wait()
-
-    for h in range(4):
-        for i in range(4):
-            q16[4 * h + i : 4 * h + i + 1, :] = q_ref[i, h : h + 1, :].astype(jnp.float32)
-    q = q16[...].astype(jnp.bfloat16)
-    kn, vn = kn_ref[...], vn_ref[...]
-    sm = 1.0 / math.sqrt(HEAD)
-    keys = kpool[...].reshape(8 * BLOCK, HEAD)
-    dims = (((1,), (1,)), ((), ()))
-    scores = lax.dot_general(q, keys, dims, preferred_element_type=jnp.float32) * sm
-    own4 = lax.dot_general(q, kn, dims, preferred_element_type=jnp.float32) * sm
-    req = lax.rem(lax.broadcasted_iota(jnp.int32, (16, 1), 0), 4)
-    first, second = jnp.full((16, 1), -1, jnp.int32), jnp.full((16, 1), -1, jnp.int32)
-    for i in range(4):
-        first = jnp.where(req == i, bt[0, i], first)
-        second = jnp.where(req == i, jnp.where(cb[i] > 1, bt[1, i], -1), second)
-    column = lax.broadcasted_iota(jnp.int32, (16, 8 * BLOCK), 1) // BLOCK
-    live = (column == first) | (column == second)
-    mine = lax.broadcasted_iota(jnp.int32, (16, 4), 1) == req
-    own = jnp.sum(jnp.where(mine, own4, 0.0), axis=1, keepdims=True)
-    masked = jnp.where(live, scores, jnp.float32(-1e30))
-    top = jnp.maximum(jnp.max(masked, axis=1, keepdims=True), own)
-    expo = jnp.where(live, jnp.exp(masked - top), 0.0)
-    self_expo = jnp.exp(own - top)
-    total = jnp.sum(expo, axis=1, keepdims=True) + self_expo
-    weights = (expo / total).astype(jnp.bfloat16)
-    self_weight = jnp.where(mine, self_expo / total, 0.0).astype(jnp.bfloat16)
-    mixed = jnp.dot(
-        weights, vpool[...].reshape(8 * BLOCK, HEAD), preferred_element_type=jnp.float32
-    ) + jnp.dot(self_weight, vn, preferred_element_type=jnp.float32)
-    attn = jnp.concatenate([mixed[4 * h : 4 * h + 4] for h in range(4)], axis=1).astype(
-        jnp.bfloat16
-    )
-
-    pltpu.make_async_copy(
-        table.at[pl.ds(0, R - 1)], table.at[pl.ds(0, R - 1)], meta_sem.at[1]
-    ).wait()
-    info_v[...] = jnp.sum(table[...], axis=0)
-    info_copy = pltpu.make_async_copy(info_v, info_s, info_sem)
-    info_copy.start()
-
-    copies[9].wait()
-    CW = levels.shape[1] // T
-
-    @pl.loop(0, T)
+    @pl.loop(0, Z)
     def _(i):
-        to = lax.rem(tp + 1 + i, T)
-        part = jnp.dot(
-            attn,
-            levels[:, pl.ds(pl.multiple_of(to * CW, CW), CW)],
-            preferred_element_type=jnp.float32,
-        )
-        piece = jnp.concatenate(
-            [part[:, 128 * k : 128 * k + 128] for k in range(CW // 128)], axis=0
-        )
-        rs_tx[to] = piece.astype(jnp.bfloat16)
-
-        @pl.when(i < T - 1)
+        peers = plane(farthest_first(i))
+        for to in peers[:-1]:
+            scatter(to)
+
+        @pl.when(i < Z - 1)
         def _():
+            scatter(peers[-1])
+
+    @pl.when(jnp.logical_not(early))
+    def _():
+        compute()
+        reduce_scatter()
+
+    collects = lax.rem(me, X) == my_x
+
+    @pl.when(collects)
+    def _():
+        pltpu.make_async_copy(
+            table.at[pl.ds(0, R - 1)], table.at[pl.ds(0, R - 1)], meta_sem.at[1]
+        ).wait()
+        info_v[...] = jnp.minimum(jnp.sum(table[...], axis=0), R - 1)
+
+        @pl.loop(1, X)
+        def _(i):
             pltpu.make_async_remote_copy(
-                src_ref=rs_tx.at[to],
-                dst_ref=rs_rx.at[tp],
-                send_sem=rs_sem.at[0],
-                recv_sem=rs_sem.at[1],
-                device_id={"tp": to},
+                src_ref=info_v,
+                dst_ref=info_v,
+                send_sem=info_sem.at[0],
+                recv_sem=info_sem.at[1],
+                device_id={"tp": tp - my_x + lax.rem(my_x + i, X)},
                 device_id_type=MESH,
             ).start()
 
-    rs_rx[tp] = rs_tx[tp]
+    pl.when(early)(finish_hidden)
+
+    @pl.when(jnp.logical_not(collects))
+    def _():
+        pltpu.make_async_copy(info_v, info_v, info_sem.at[1]).wait()
+
+    info_copy = pltpu.make_async_copy(info_v, info_s, info_sem.at[2])
+    info_copy.start()
 
     info_copy.wait()
     pltpu.make_async_copy(
@@ -243,10 +352,7 @@
     my_k = lax.rem(my_t, per_block)
 
     def deliver(out):
-        @pl.loop(1, R)
-        def _(i):
-            to = lax.rem(me + i, R)
-            tx2[to] = rx1[lax.rem(info_s[0, 64 * my_j + to] // 4, R)]
+        def send(to):
             pltpu.make_async_remote_copy(
                 src_ref=tx2.at[to],
                 dst_ref=out.at[my_j, my_b, 0, my_k],
@@ -256,7 +362,19 @@
                 device_id_type=MESH,
             ).start()
 
-        tx2[me] = rx1[lax.rem(info_s[0, 64 * my_j + me] // 4, R)]
+        @pl.loop(0, Z)
+        def _(z):
+            peers = plane(z)
+            pieces = [rx1[info_s[0, 64 * my_j + to]] for to in peers]
+            for to, piece in zip(peers, pieces):
+                tx2[to] = piece
+            for to in peers[:-1]:
+                send(to)
+
+            @pl.when(z != my_z)
+            def _():
+                send(peers[-1])
+
         pltpu.make_async_copy(tx2.at[me], out.at[my_j, my_b, 0, my_k], out_sem.at[4]).start()
 
     @pl.when(my_t < half // 2)
@@ -268,46 +386,22 @@
         deliver(rv_ref)
 
     for j in range(2):
-        word = info_s[0, 64 * j + me]
-        src_ref[j] = word // 4
-        cnt_ref[j] = lax.rem(word, 4)
+        src_ref[j] = info_s[0, 64 * j + me]
+        cnt_ref[j] = info_s[1, 64 * j + me]
     small = [
         pltpu.make_async_copy(cnt_ref, cnt_out, out_sem.at[0]),
         pltpu.make_async_copy(src_ref, src_out, out_sem.at[1]),
     ]
     for c in small:
         c.start()
-    for c in copies[10:]:
-        c.wait()
-
-    pltpu.make_async_copy(
-        rs_rx.at[pl.ds(0, T - 1)], rs_rx.at[pl.ds(0, T - 1)], rs_sem.at[1]
-    ).wait()
-    sixteen = jnp.sum(rs_rx[...].astype(jnp.float32), axis=0)
-    summed = jnp.concatenate([sixteen[4 * k : 4 * k + 4] for k in range(CW // 128)], axis=1)
-    hidden = (summed * scale_ref[...] + res_ref[...].astype(jnp.float32)).astype(jnp.bfloat16)
-    hid_ref[...] = hidden
-    small.append(pltpu.make_async_copy(hid_ref, hid_out, out_sem.at[2]))
-    small[-1].start()
-    wide = hidden.astype(jnp.float32)
-    square = jnp.sum(wide * wide, axis=1, keepdims=True)
-    ss_tx[...] = jnp.broadcast_to(square, (4, 128))
-    ss_rx[tp] = ss_tx[...]
-
-    @pl.loop(1, T)
-    def _(i):
-        pltpu.make_async_remote_copy(
-            src_ref=ss_tx,
-            dst_ref=ss_rx.at[tp],
-            send_sem=ss_sem.at[0],
-            recv_sem=ss_sem.at[1],
-            device_id={"tp": lax.rem(tp + i, T)},
-            device_id_type=MESH,
-        ).start()
+
+    small.append(hid_copy)
+    pl.when(jnp.logical_not(early))(finish_hidden)
 
     pltpu.make_async_copy(
         ss_rx.at[pl.ds(0, T - 1)], ss_rx.at[pl.ds(0, T - 1)], ss_sem.at[1]
     ).wait()
+    wide = hid_ref[...].astype(jnp.float32)
     mean = jnp.sum(ss_rx[...], axis=0)[:, 0:1] / (CW * T)
     norm_ref[...] = (wide * lax.rsqrt(mean + 1e-5) * gain_ref[...]).astype(jnp.bfloat16)
 
@@ -321,11 +415,21 @@
         (rx1, R - 1, mig_sem.at[0]),
         (rx1, R - 1, mig_sem.at[2]),
         (rx1, R - 1, mig_sem.at[3]),
-        (table, R - 1, meta_sem.at[0]),
         (rs_tx, T - 1, rs_sem.at[0]),
         (ss_rx, T - 1, ss_sem.at[0]),
     ):
         pltpu.make_async_copy(buf.at[pl.ds(0, count)], buf.at[pl.ds(0, count)], sem).wait()
+
+    @pl.when(collects)
+    def _():
+        for count, sem in ((R // X - 1, meta_sem.at[0]), (X - 1, info_sem.at[0])):
+            pltpu.make_async_copy(table.at[pl.ds(0, count)], table.at[pl.ds(0, count)], sem).wait()
+
+    @pl.when(jnp.logical_not(collects))
+    def _():
+        pltpu.make_async_copy(
+            table.at[pl.ds(0, R // X)], table.at[pl.ds(0, R // X)], meta_sem.at[0]
+        ).wait()
 
 
 def emit(n, *refs):
@@ -386,9 +490,9 @@
                 pltpu.VMEM((2, R // 2, CR, HEAD), bf16),
                 pltpu.VMEM((R, CR, HEAD), bf16),
                 pltpu.VMEM((R, CR, HEAD), bf16),
-                pltpu.VMEM((R, 1, 128), i32),
-                pltpu.VMEM((1, 128), i32),
-                pltpu.SMEM((1, 128), i32),
+                pltpu.VMEM((R, 2, 128), i32),
+                pltpu.VMEM((2, 128), i32),
+                pltpu.SMEM((2, 128), i32),
                 pltpu.VMEM((T, 4 * CW // 128, 128), bf16),
                 pltpu.VMEM((T, 4 * CW // 128, 128), bf16),
                 pltpu.VMEM((4, 128), f32),
@@ -396,7 +500,7 @@
                 pltpu.SemaphoreType.DMA((13,)),
                 pltpu.SemaphoreType.DMA((4,)),
                 pltpu.SemaphoreType.DMA((2,)),
-                pltpu.SemaphoreType.DMA,
+                pltpu.SemaphoreType.DMA((3,)),
                 pltpu.SemaphoreType.DMA((2,)),
                 pltpu.SemaphoreType.DMA((2,)),
                 pltpu.SemaphoreType.DMA((5,)),

time: 42.5 us -> 39.5 us (0.929)
  Pallas kernels: 41.7 us -> 38.8 us
    pallas_call x1, Pallas kernels: 39.9 us -> 37 us  [shards(): pl.pallas_call(functools.partial(body, R, T), out_shape=(jax.ShapeDtypeSt...]
where the time goes in v3:
time: 39.5 us; the launch traced here: 39.4 us
  Pallas kernels  38.8 us (98%)
  between operations  0.65 us (2%)
    pallas_call x1, Pallas kernels, shards(): pl.pallas_call(functools.partial(body, R, T), out_shape=(jax.ShapeDtypeSt...  37 us
    pallas_call x1, Pallas kernels, shards(): pl.pallas_call(functools.partial(emit, 6), out_shape=tuple((jax.ShapeDtyp...  1.74 us

profile of v3, /device:TPU:1, one launch (start us, length us, event | category | flops | bytes accessed | tf_op | source)
XLA Modules:
  0.0 39.4 jit_solution(17231819673276169366)
XLA Ops:
  0.6 37.0 %decode_and_migrate.1 = (bf16[4,512]{1,0:T(4,128)(2,1)}, bf16[4,512]{1,0:T(4,128)(2,1)}, bf16[2,2,1,8,16,128]{5,4,3,2,1,0:T(8,128)(2,1)}, bf16[2,2,1,8,16,128]{5...) custom-call(s32[2,4]{1,0:T(2,128)} %bitcast.13, s32[4]{0:T(128)} %cb_hbm.1, s32[2]{0:T(128)} %mreq_hbm.1, s32[2]{0:T(128)} %mdest_hbm.1, ...), custom_call_target="tpu_custom_call" | custom-call | tf_op jit(solution)/shard_map/decode_and_migrate/pallas_call | solution.py:459
  37.7 1.7 %write_outputs.1 = (bf16[4,512]{1,0:T(4,128)(2,1)}, bf16[4,512]{1,0:T(4,128)(2,1)}, bf16[2,2,1,8,16,128]{5,4,3,2,1,0:T(8,128)(2,1)}, bf16[2,2,1,8,16,128]{5,4,3,...) custom-call(bf16[4,512]{1,0:T(4,128)(2,1)} %get-tuple-element.18.refs_0_, bf16[4,512]{1,0:T(4,128)(2,1)} %get-tuple-element.19.refs_1_, ...), custom_call_target="tpu_custom_call" | custom-call | tf_op jit(solution)/shard_map/write_outputs/pallas_call | solution.py:527

commit v4 on v3

--- a/solution.py
+++ b/solution.py
@@ -65,8 +65,9 @@
     stage,
     rx1,
     tx2,
+    row,
     table,
-    info_v,
+    info,
     info_s,
     rs_tx,
     rs_rx,
@@ -85,8 +86,6 @@
     CR = 2 * ROWS // R
     per_block = BLOCK // CR
     half = R // 2
-    X = min(4, T)
-    my_x = lax.rem(tp, X)
     Z = min(8, R // 2)
     Y = R // (2 * Z)
     my_y, my_z, core = me // (2 * Z), lax.rem(me // 2, Z), lax.rem(me, 2)
@@ -149,13 +148,12 @@
     for c in copies[:4]:
         c.wait()
 
-    lane = lax.broadcasted_iota(jnp.int32, (2, 128), 1)
-    kind = lax.broadcasted_iota(jnp.int32, (2, 128), 0)
+    lane = lax.broadcasted_iota(jnp.int32, (1, 128), 1)
     r0, r1 = mreq[0], mreq[1]
     c0, c1 = cb[r0], cb[r1]
-    table[me] = jnp.where(lane == mdest[0], jnp.where(kind == 0, me, c0), 0) + jnp.where(
-        lane == 64 + mdest[1], jnp.where(kind == 0, me, c1), 0
-    )
+    for j, c in enumerate((c0, c1)):
+        row[j] = jnp.where(lane == mdest[j], me, 0) + jnp.where(lane == 64 + mdest[j], c, 0)
+    table[me] = row[core]
     copies[4].wait()
     copies[5].wait()
     for j, (r, c) in enumerate(((r0, c0), (r1, c1))):
@@ -275,20 +273,15 @@
 
     pl.when(early)(reduce_scatter)
 
-    @pl.loop(0, R // X)
-    def _(i):
-        to = i * X + my_x
-
-        @pl.when(to != me)
-        def _():
-            pltpu.make_async_remote_copy(
-                src_ref=table.at[me],
-                dst_ref=table.at[me],
-                send_sem=meta_sem.at[0],
-                recv_sem=meta_sem.at[1],
-                device_id={"replica": to},
-                device_id_type=MESH,
-            ).start()
+    def announce(to):
+        pltpu.make_async_remote_copy(
+            src_ref=row.at[lax.rem(to, 2)],
+            dst_ref=table.at[me],
+            send_sem=meta_sem.at[0],
+            recv_sem=meta_sem.at[1],
+            device_id={"replica": to},
+            device_id_type=MESH,
+        ).start()
 
     def scatter(to):
         pltpu.make_async_remote_copy(
@@ -304,6 +297,16 @@
     def _(i):
         peers = plane(farthest_first(i))
         for to in peers[:-1]:
+            announce(to)
+
+        @pl.when(i < Z - 1)
+        def _():
+            announce(peers[-1])
+
+    @pl.loop(0, Z)
+    def _(i):
+        peers = plane(farthest_first(i))
+        for to in peers[:-1]:
             scatter(to)
 
         @pl.when(i < Z - 1)
@@ -315,34 +318,23 @@
         compute()
         reduce_scatter()
 
-    collects = lax.rem(me, X) == my_x
-
-    @pl.when(collects)
-    def _():
-        pltpu.make_async_copy(
-            table.at[pl.ds(0, R - 1)], table.at[pl.ds(0, R - 1)], meta_sem.at[1]
-        ).wait()
-        info_v[...] = jnp.minimum(jnp.sum(table[...], axis=0), R - 1)
-
-        @pl.loop(1, X)
-        def _(i):
-            pltpu.make_async_remote_copy(
-                src_ref=info_v,
-                dst_ref=info_v,
-                send_sem=info_sem.at[0],
-                recv_sem=info_sem.at[1],
-                device_id={"tp": tp - my_x + lax.rem(my_x + i, X)},
-                device_id_type=MESH,
-            ).start()
-
     pl.when(early)(finish_hidden)
 
-    @pl.when(jnp.logical_not(collects))
-    def _():
-        pltpu.make_async_copy(info_v, info_v, info_sem.at[1]).wait()
-
-    info_copy = pltpu.make_async_copy(info_v, info_s, info_sem.at[2])
+    pltpu.make_async_copy(
+        table.at[pl.ds(0, R - 1)], table.at[pl.ds(0, R - 1)], meta_sem.at[1]
+    ).wait()
+    info[0] = jnp.minimum(jnp.sum(table[...], axis=0), R - 1)
+    info_copy = pltpu.make_async_copy(info.at[0], info_s.at[0], info_sem.at[0])
     info_copy.start()
+    swap = pltpu.make_async_remote_copy(
+        src_ref=info.at[0],
+        dst_ref=info.at[1],
+        send_sem=info_sem.at[1],
+        recv_sem=info_sem.at[2],
+        device_id={"replica": me + 1 - 2 * core},
+        device_id_type=MESH,
+    )
+    swap.start()
 
     info_copy.wait()
     pltpu.make_async_copy(
@@ -365,7 +357,7 @@
         @pl.loop(0, Z)
         def _(z):
             peers = plane(z)
-            pieces = [rx1[info_s[0, 64 * my_j + to]] for to in peers]
+            pieces = [rx1[info_s[0, 0, to]] for to in peers]
             for to, piece in zip(peers, pieces):
                 tx2[to] = piece
             for to in peers[:-1]:
@@ -385,9 +377,14 @@
     def _():
         deliver(rv_ref)
 
+    swap.wait()
+    swap_copy = pltpu.make_async_copy(info.at[1], info_s.at[1], info_sem.at[3])
+    swap_copy.start()
+    swap_copy.wait()
     for j in range(2):
-        src_ref[j] = info_s[0, 64 * j + me]
-        cnt_ref[j] = info_s[1, 64 * j + me]
+        k = jnp.where(core == j, 0, 1)
+        src_ref[j] = info_s[k, 0, me]
+        cnt_ref[j] = info_s[k, 0, 64 + me]
     small = [
         pltpu.make_async_copy(cnt_ref, cnt_out, out_sem.at[0]),
         pltpu.make_async_copy(src_ref, src_out, out_sem.at[1]),
@@ -417,19 +414,9 @@
         (rx1, R - 1, mig_sem.at[3]),
         (rs_tx, T - 1, rs_sem.at[0]),
         (ss_rx, T - 1, ss_sem.at[0]),
+        (table, R - 1, meta_sem.at[0]),
     ):
         pltpu.make_async_copy(buf.at[pl.ds(0, count)], buf.at[pl.ds(0, count)], sem).wait()
-
-    @pl.when(collects)
-    def _():
-        for count, sem in ((R // X - 1, meta_sem.at[0]), (X - 1, info_sem.at[0])):
-            pltpu.make_async_copy(table.at[pl.ds(0, count)], table.at[pl.ds(0, count)], sem).wait()
-
-    @pl.when(jnp.logical_not(collects))
-    def _():
-        pltpu.make_async_copy(
-            table.at[pl.ds(0, R // X)], table.at[pl.ds(0, R // X)], meta_sem.at[0]
-        ).wait()
 
 
 def emit(n, *refs):
@@ -490,9 +477,10 @@
                 pltpu.VMEM((2, R // 2, CR, HEAD), bf16),
                 pltpu.VMEM((R, CR, HEAD), bf16),
                 pltpu.VMEM((R, CR, HEAD), bf16),
-                pltpu.VMEM((R, 2, 128), i32),
-                pltpu.VMEM((2, 128), i32),
-                pltpu.SMEM((2, 128), i32),
+                pltpu.VMEM((2, 1, 128), i32),
+                pltpu.VMEM((R, 1, 128), i32),
+                pltpu.VMEM((2, 1, 128), i32),
+                pltpu.SMEM((2, 1, 128), i32),
                 pltpu.VMEM((T, 4 * CW // 128, 128), bf16),
                 pltpu.VMEM((T, 4 * CW // 128, 128), bf16),
                 pltpu.VMEM((4, 128), f32),
@@ -500,7 +488,7 @@
                 pltpu.SemaphoreType.DMA((13,)),
                 pltpu.SemaphoreType.DMA((4,)),
                 pltpu.SemaphoreType.DMA((2,)),
-                pltpu.SemaphoreType.DMA((3,)),
+                pltpu.SemaphoreType.DMA((4,)),
                 pltpu.SemaphoreType.DMA((2,)),
                 pltpu.SemaphoreType.DMA((2,)),
                 pltpu.SemaphoreType.DMA((5,)),

time: 39.5 us -> 38.3 us (0.970)
  Pallas kernels: 38.8 us -> 37.5 us
    pallas_call x1, Pallas kernels: 37 us -> 35.7 us  [shards(): pl.pallas_call(functools.partial(body, R, T), out_shape=(jax.ShapeDtypeSt...]
where the time goes in v4:
time: 38.3 us; the launch traced here: 38.1 us
  Pallas kernels  37.5 us (98%)
  between operations  0.65 us (2%)
    pallas_call x1, Pallas kernels, shards(): pl.pallas_call(functools.partial(body, R, T), out_shape=(jax.ShapeDtypeSt...  35.7 us
    pallas_call x1, Pallas kernels, shards(): pl.pallas_call(functools.partial(emit, 6), out_shape=tuple((jax.ShapeDtyp...  1.74 us

profile of v4, /device:TPU:1, one launch (start us, length us, event | category | flops | bytes accessed | tf_op | source)
XLA Modules:
  0.0 38.1 jit_solution(10344411429760991381)
XLA Ops:
  0.6 35.7 %decode_and_migrate.1 = (bf16[4,512]{1,0:T(4,128)(2,1)}, bf16[4,512]{1,0:T(4,128)(2,1)}, bf16[2,2,1,8,16,128]{5,4,3,2,1,0:T(8,128)(2,1)}, bf16[2,2,1,8,16,128]{5...) custom-call(s32[2,4]{1,0:T(2,128)} %bitcast.13, s32[4]{0:T(128)} %cb_hbm.1, s32[2]{0:T(128)} %mreq_hbm.1, s32[2]{0:T(128)} %mdest_hbm.1, ...), custom_call_target="tpu_custom_call" | custom-call | tf_op jit(solution)/shard_map/decode_and_migrate/pallas_call | solution.py:446
  36.4 1.7 %write_outputs.1 = (bf16[4,512]{1,0:T(4,128)(2,1)}, bf16[4,512]{1,0:T(4,128)(2,1)}, bf16[2,2,1,8,16,128]{5,4,3,2,1,0:T(8,128)(2,1)}, bf16[2,2,1,8,16,128]{5,4,3,...) custom-call(bf16[4,512]{1,0:T(4,128)(2,1)} %get-tuple-element.18.refs_0_, bf16[4,512]{1,0:T(4,128)(2,1)} %get-tuple-element.19.refs_1_, ...), custom_call_target="tpu_custom_call" | custom-call | tf_op jit(solution)/shard_map/write_outputs/pallas_call | solution.py:515

commit v5 on v4

--- a/solution.py
+++ b/solution.py
@@ -305,11 +305,12 @@
 
     @pl.loop(0, Z)
     def _(i):
-        peers = plane(farthest_first(i))
+        z = Z - 1 - i
+        peers = plane(z)
         for to in peers[:-1]:
             scatter(to)
 
-        @pl.when(i < Z - 1)
+        @pl.when(z != my_z)
         def _():
             scatter(peers[-1])
 

time: 38.3 us -> 37.5 us (0.979)
  Pallas kernels: 37.5 us -> 36.7 us
    pallas_call x1, Pallas kernels: 35.7 us -> 34.9 us  [shards(): pl.pallas_call(functools.partial(body, R, T), out_shape=(jax.ShapeDtypeSt...]
where the time goes in v5:
time: 37.5 us; the launch traced here: 37.3 us
  Pallas kernels  36.7 us (98%)
  between operations  0.65 us (2%)
    pallas_call x1, Pallas kernels, shards(): pl.pallas_call(functools.partial(body, R, T), out_shape=(jax.ShapeDtypeSt...  34.9 us
    pallas_call x1, Pallas kernels, shards(): pl.pallas_call(functools.partial(emit, 6), out_shape=tuple((jax.ShapeDtyp...  1.74 us

profile of v5, /device:TPU:1, one launch (start us, length us, event | category | flops | bytes accessed | tf_op | source)
XLA Modules:
  0.0 37.3 jit_solution(13085563528032694336)
XLA Ops:
  0.6 34.9 %decode_and_migrate.1 = (bf16[4,512]{1,0:T(4,128)(2,1)}, bf16[4,512]{1,0:T(4,128)(2,1)}, bf16[2,2,1,8,16,128]{5,4,3,2,1,0:T(8,128)(2,1)}, bf16[2,2,1,8,16,128]{5...) custom-call(s32[2,4]{1,0:T(2,128)} %bitcast.13, s32[4]{0:T(128)} %cb_hbm.1, s32[2]{0:T(128)} %mreq_hbm.1, s32[2]{0:T(128)} %mdest_hbm.1, ...), custom_call_target="tpu_custom_call" | custom-call | tf_op jit(solution)/shard_map/decode_and_migrate/pallas_call | solution.py:447
  35.6 1.7 %write_outputs.1 = (bf16[4,512]{1,0:T(4,128)(2,1)}, bf16[4,512]{1,0:T(4,128)(2,1)}, bf16[2,2,1,8,16,128]{5,4,3,2,1,0:T(8,128)(2,1)}, bf16[2,2,1,8,16,128]{5,4,3,...) custom-call(bf16[4,512]{1,0:T(4,128)(2,1)} %get-tuple-element.18.refs_0_, bf16[4,512]{1,0:T(4,128)(2,1)} %get-tuple-element.19.refs_1_, ...), custom_call_target="tpu_custom_call" | custom-call | tf_op jit(solution)/shard_map/write_outputs/pallas_call | solution.py:516
